TPU v7x, 512 devices: a whole 4x4x16 slice. The times are simulated.
512 devices in a mesh: queue: 16 (over z_lo, core), heads: 32 (over x, z_hi, y).
Axes of the slice: x: 4, y: 4, z: 16 (z_hi: 2, z_lo: 8; z = z_hi * 8 + z_lo), core: 2. Of those that a mesh axis runs over, the one named last changes fastest.
Arguments:
- state: bfloat16 [65536, 4096], P(('queue', 'heads')), may hold values from -10 to 10
- fresh: bfloat16 [1, 4096, 4096], P(None, 'heads'), may hold values from -6 to 6
- frame_level: int32 [2, 256], P(None, 'queue'), may hold values from 0 to 47
- request: int32 [2, 16], P(None, 'queue'), may hold values from 0 to 3
- q_table: float32 [48, 4096], P(None, 'heads'), may hold values from -4.5 to 4.5
- k_table: float32 [48, 4096], P(None, 'heads'), may hold values from -4.5 to 4.5
- step_size: float32 [48], replicated, may hold values from 0.2 to 1
- reference_kv: bfloat16 [2, 4, 256, 4096], P(None, None, None, 'heads'), may hold values from -6 to 6
Outputs:
- final_state: bfloat16 [65536, 4096], P(('queue', 'heads'))
All inputs are finite; a program needn't handle non-finite values.
Results may differ from a plain program's by a relative error of at most 0.0053.
Values may be sent and summed in bfloat16 or wider, within the bound.
A program may use at most 64 MiB of HBM per device.

v0:
```python
import jax
import jax.numpy as jnp
from jax import lax
from jax.sharding import PartitionSpec as P

FT = 256
FRAMES = 16
ITERS = 2


epsilon = 1e-06
far_below = -1e30


def passed_along(array, axis, by):
    length = lax.axis_size(axis)
    pairs = [(i, i + by) for i in range(length) if 0 <= i + by < length]
    return lax.ppermute(array, axis, pairs)


def frame_attention(queries, key_rows, values, has_prev, has_next, ref_keys, ref_values):
    head_width = queries.shape[1]
    frames = queries.shape[0] // FT
    groups = frames // 2
    key_pairs = key_rows.reshape(groups + 1, 2 * FT, head_width)
    val_pairs = values.reshape(groups + 1, 2 * FT, head_width)
    key_window = jnp.concatenate([key_pairs[:-1], key_pairs[1:]], axis=1)
    val_window = jnp.concatenate([val_pairs[:-1], val_pairs[1:]], axis=1)
    query_groups = queries.reshape(groups, 2 * FT, head_width)
    row_frame = (jnp.arange(2 * FT) // FT)[:, None]
    col_frame = (jnp.arange(4 * FT) // FT)[None, :]
    offset = col_frame - row_frame
    in_window = jnp.logical_and(offset >= 0, offset <= 2)
    scale = 1.0 / head_width**0.5

    def one_group(inputs):
        group_q, group_k, group_v, group_id = inputs
        first_ok = jnp.logical_or(group_id > 0, has_prev)
        last_ok = jnp.logical_or(group_id < groups - 1, has_next)
        edge_ok = jnp.logical_and(
            jnp.logical_or(col_frame != 0, first_ok), jnp.logical_or(col_frame != 3, last_ok)
        )
        allowed = jnp.logical_and(in_window, edge_ok)
        local_scores = jnp.dot(group_q, group_k.T, preferred_element_type=jnp.float32) * scale
        local_scores = jnp.where(allowed, local_scores, far_below)
        remote = jnp.dot(group_q, ref_keys.T, preferred_element_type=jnp.float32) * scale
        row_max = jnp.maximum(jnp.max(local_scores, axis=1), jnp.max(remote, axis=1))[:, None]
        probs_local = jnp.exp(local_scores - row_max)
        probs_remote = jnp.exp(remote - row_max)
        denominator = (jnp.sum(probs_local, axis=1) + jnp.sum(probs_remote, axis=1))[:, None]
        weight_local = (probs_local / denominator).astype(jnp.bfloat16)
        weight_remote = (probs_remote / denominator).astype(jnp.bfloat16)
        result = jnp.dot(weight_local, group_v, preferred_element_type=jnp.float32)
        result = result + jnp.dot(weight_remote, ref_values, preferred_element_type=jnp.float32)
        return result.astype(jnp.bfloat16)

    results = lax.map(one_group, (query_groups, key_window, val_window, jnp.arange(groups)))
    return results.reshape(groups * 2 * FT, head_width)


def local(state, fresh, frame_level, request, q_table, k_table, step_size, reference_kv):
    head_width = q_table.shape[1]
    queue_pos = lax.axis_index("queue")
    queue_len = lax.axis_size("queue")
    head_pos = lax.axis_index("heads")
    own_rows = state.shape[0]
    block_len = FRAMES * FT
    has_prev = queue_pos > 0
    has_next = queue_pos < queue_len - 1
    level_ids = jnp.arange(q_table.shape[0])
    current = state
    for sweep in range(ITERS):
        as_float = current.astype(jnp.float32)
        own_scale = lax.rsqrt(jnp.mean(as_float * as_float, axis=1) + epsilon)
        row_scale = lax.all_gather(own_scale, "heads", axis=0, tiled=True)
        head_state = lax.all_to_all(current, "heads", split_axis=1, concat_axis=0, tiled=True)
        one_hot = (frame_level[sweep][:, None] == level_ids[None, :]).astype(jnp.float32)
        q_scale = jnp.dot(one_hot, q_table, precision=lax.Precision.HIGHEST)
        k_scale = jnp.dot(one_hot, k_table, precision=lax.Precision.HIGHEST)
        step_frame = jnp.dot(one_hot, step_size[:, None], precision=lax.Precision.HIGHEST)[:, 0]
        normed = head_state.astype(jnp.float32).reshape(FRAMES, FT, head_width) * row_scale.reshape(
            FRAMES, FT, 1
        )
        queries = (normed * q_scale[:, None, :]).astype(jnp.bfloat16).reshape(block_len, head_width)
        key_rows = (
            (normed * k_scale[:, None, :]).astype(jnp.bfloat16).reshape(block_len, head_width)
        )
        key_value = jnp.stack([key_rows, head_state])
        before = passed_along(key_value[:, block_len - FT :], "queue", 1)
        after_rim = passed_along(key_value[:, :FT], "queue", -1)
        padded = jnp.concatenate([before, key_value, after_rim], axis=1)
        chosen = lax.dynamic_index_in_dim(reference_kv, request[sweep, 0], 1, keepdims=False)
        attn = frame_attention(
            queries, padded[0], padded[1], has_prev, has_next, chosen[0], chosen[1]
        )
        attn, step_rows = (attn, jnp.repeat(step_frame, FT))
        back = lax.all_to_all(attn, "heads", split_axis=0, concat_axis=1, tiled=True)
        mine = lax.dynamic_slice_in_dim(step_rows, head_pos * own_rows, own_rows)
        current = (as_float + mine[:, None] * back.astype(jnp.float32)).astype(jnp.bfloat16)
        if sweep < ITERS - 1:
            shifted = passed_along(current, "queue", 1)
            current = jnp.where(has_prev, shifted, fresh[sweep])
    return current


def solution(mesh):
    placed = (
        P(("queue", "heads"), None),
        P(None, "heads", None),
        P(None, "queue"),
        P(None, "queue"),
        P(None, "heads"),
        P(None, "heads"),
        P(),
        P(None, None, None, "heads"),
    )
    return jax.shard_map(
        local, mesh=mesh, in_specs=placed, out_specs=P(("queue", "heads"), None), check_vma=False
    )
```

profile of v0, /device:TPU:33, one launch (start us, length us, event | category | flops | bytes accessed | tf_op | source)
XLA Modules:
  0.0 665.5 jit_solution(6820676645958053562)
XLA Ops:
  0.0 2.6 copy_bitcast_fusion
  2.6 19.5 %all-to-all-start = ((bf16[128,32,128]{2,0,1:T(8,128)(2,1)}), bf16[128,32,128]{2,0,1:T(8,128)(2,1)S(1)}, u32[]{:S(2)}, u32[]{:S(2)}) async-start(bf16[128,32,128]{2,0,1:T(8,128)(2,1)} %copy_bitcast_fusion), calls=%async_computation | async-start | bytes 2097152 | tf_op jit(solution)/shard_map/all_to_all | solution.py:76
  26.6 169.8 %all-gather = f32[32,1,128]{2,1,0:T(1,128)S(1)} all-gather(f32[1,1,128]{2,1,0:T(1,128)S(1)} %rsqrt_bitcast_fusion.1), channel_id=1, replica_groups=mesh['queue'=16,'heads'=32] {'heads'}, dimensions={0}, use_global_device_ids=true | all-gather | bytes 16896 | tf_op jit(solution)/shard_map/all_gather | solution.py:75
  198.8 1.6 dynamic-slice_bitcast_fusion
  201.8 5.2 collective-permute-start
  207.1 13.4 %collective-permute-start.1 = (bf16[2,256,128]{2,1,0:T(8,128)(2,1)S(1)}, bf16[2,256,128]{2,1,0:T(8,128)(2,1)S(1)}, u32[]{:S(2)}, u32[]{:S(2)}) collective-permute-start(bf16[2,256,128]{2,1,0:T(8,128)(2,1)S(1)} %get-tuple-element.324), channel_id=1, source_target_pairs={{32,0},{64,32},{96,64},{128,96},{160,128},{192,160},{224,192},{256... | collective-permute-start | bytes 393224 | tf_op jit(solution)/shard_map/ppermute | solution.py:18
  221.4 4.4 pad_maximum_fusion.12
  225.8 2.2 pad_maximum_fusion
  228.2 51.9 %while.24 = (s32[]{:T(128)}, bf16[8,512,128]{2,1,0:T(8,128)(2,1)S(1)}, s32[8]{0:T(128)S(1)}, pred[]{:T(512)}, pred[]{:T(512)}, /*index=5*/bf16[8,512,128]{2,1,0:...) while((s32[]{:T(128)}, ...), condition=%wide.region_6.7_spmd.clone.clone, body=%wide.region_1.6_spmd.clone.clone.sunk | while | flops 343420928 | bytes 9479867 | solution.py:57
  230.2 1.8 fusion.112
  232.9 1.5 fusion.116
  236.7 1.8 fusion.112
  239.4 1.5 fusion.116
  243.2 1.8 fusion.112
  245.9 1.5 fusion.116
  249.6 1.8 fusion.112
  252.4 1.5 fusion.116
  256.1 1.8 fusion.112
  258.9 1.5 fusion.116
  262.6 1.8 fusion.112
  265.4 1.5 fusion.116
  269.1 1.8 fusion.112
  275.6 1.8 fusion.112
  278.4 1.5 fusion.116
  281.5 3.9 all-to-all-start.1
  285.8 44.0 %all-to-all-done.1 = bf16[32,128,128]{1,2,0:T(8,128)(2,1)S(1)} async-done(((bf16[32,128,128]{1,2,0:T(8,128)(2,1)}), bf16[32,128,128]{1,2,0:T(8,128)(2,1)S(1)}, u32[]{:S(2)}, u32[]{:S(2)}) %all-to-all-start.1) | async-done | bytes 1048608 | tf_op jit(solution)/shard_map/all_to_all | solution.py:97
  331.1 1.9 collective-permute-start.2
  333.7 11.4 %collective-permute-done.2 = bf16[128,4096]{0,1:T(8,128)(2,1)S(1)} collective-permute-done((bf16[128,4096]{0,1:T(8,128)(2,1)}, bf16[128,4096]{0,1:T(8,128)(2,1)S(1)}, u32[]{:S(2)}, u32[]{:S(2)}) %collective-permute-start.2) | collective-permute-done | bytes 1048608 | tf_op jit(solution)/shard_map/ppermute | solution.py:18
  346.5 4.7 all-to-all-start.2
  351.6 167.7 %all-gather.1 = f32[32,1,128]{2,1,0:T(1,128)S(1)} all-gather(f32[1,1,128]{2,1,0:T(1,128)S(1)} %rsqrt_bitcast_fusion), channel_id=1, replica_groups=mesh['queue'=16,'heads'=32] {'heads'}, dimensions={0}, use_global_device_ids=true | all-gather | bytes 16896 | tf_op jit(solution)/shard_map/all_gather | solution.py:75
  522.3 3.7 collective-permute-start.3
  526.0 15.6 %collective-permute-start.4 = (bf16[2,256,128]{2,1,0:T(8,128)(2,1)}, bf16[2,256,128]{2,1,0:T(8,128)(2,1)S(1)}, u32[]{:S(2)}, u32[]{:S(2)}) collective-permute-start(bf16[2,256,128]{2,1,0:T(8,128)(2,1)} %get-tuple-element.320), channel_id=1, source_target_pairs={{32,0},{64,32},{96,64},{128,96},{160,128},{192,160},{224,192},{256... | collective-permute-start | bytes 393224 | tf_op jit(solution)/shard_map/ppermute | solution.py:18
  541.6 1.6 bitcast_convert_fusion
  543.2 2.9 copy.35
  549.2 4.5 pad_maximum_fusion.6
  553.8 1.5 pad_maximum_fusion.2
  555.5 50.2 %while.25 = (s32[]{:T(128)}, bf16[8,512,128]{2,1,0:T(8,128)(2,1)S(1)}, s32[8]{0:T(128)S(1)}, pred[]{:T(512)}, pred[]{:T(512)}, /*index=5*/bf16[8,512,128]{2,1,0:...) while((s32[]{:T(128)}, ...), condition=%wide.region_13.14_spmd.clone.clone, body=%wide.region_8.13_spmd.clone.clone.sunk | while | flops 343420928 | bytes 9479867 | solution.py:57
  557.2 1.9 fusion.121
  563.5 1.9 fusion.121
  569.7 1.9 fusion.121
  576.0 1.9 fusion.121
  582.3 1.9 fusion.121
  588.6 1.9 fusion.121
  594.8 1.9 fusion.121
  601.1 1.9 fusion.121
  607.0 3.9 all-to-all-start.3
  611.3 51.3 %all-to-all-done.3 = bf16[32,128,128]{1,2,0:T(8,128)(2,1)S(1)} async-done(((bf16[32,128,128]{1,2,0:T(8,128)(2,1)}), bf16[32,128,128]{1,2,0:T(8,128)(2,1)S(1)}, u32[]{:S(2)}, u32[]{:S(2)}) %all-to-all-start.3) | async-done | bytes 1048608 | tf_op jit(solution)/shard_map/all_to_all | solution.py:97
  662.6 1.6 fusion.53
  (208 shorter events, 62.0 us)
Async XLA Ops:
  0.0 200.4 %copy-start = (f32[48,128]{1,0:T(8,128)S(1)}, f32[48,128]{1,0:T(8,128)}, u32[]{:S(2)}) copy-start(f32[48,128]{1,0:T(8,128)} %param.17) | copy-start | bytes 73732
  0.0 22.1 %copy-start.2 = (bf16[128,4096]{1,0:T(8,128)(2,1)S(1)}, bf16[128,4096]{1,0:T(8,128)(2,1)}, u32[]{:S(2)}) copy-start(bf16[128,4096]{1,0:T(8,128)(2,1)} %param.12) | copy-start | bytes 3145732
  2.6 20.2 %copy-start.5 = (s32[2,1]{0,1:T(1,128)S(1)}, s32[2,1]{0,1:T(1,128)}, u32[]{:S(2)}) copy-start(s32[2,1]{0,1:T(1,128)} %param.15) | copy-start | bytes 28
  2.6 198.2 %all-to-all-start = ((bf16[128,32,128]{2,0,1:T(8,128)(2,1)}), bf16[128,32,128]{2,0,1:T(8,128)(2,1)S(1)}, u32[]{:S(2)}, u32[]{:S(2)}) async-start(bf16[128,32,128]{2,0,1:T(8,128)(2,1)} %copy_bitcast_fusion), calls=%async_computation | async-start | bytes 2097152 | tf_op jit(solution)/shard_map/all_to_all | solution.py:76
  22.1 178.3 %copy-start.6 = (s32[2,16]{1,0:T(2,128)S(1)}, s32[2,16]{1,0:T(2,128)}, u32[]{:S(2)}) copy-start(s32[2,16]{1,0:T(2,128)} %param.14) | copy-start | bytes 388
  22.1 178.5 %copy-start.7 = (f32[48,128]{1,0:T(8,128)S(1)}, f32[48,128]{1,0:T(8,128)}, u32[]{:S(2)}) copy-start(f32[48,128]{1,0:T(8,128)} %param.16) | copy-start | bytes 73732
  201.8 19.5 %collective-permute-start = (bf16[2,256,128]{2,1,0:T(8,128)(2,1)S(1)}, bf16[2,256,128]{2,1,0:T(8,128)(2,1)S(1)}, u32[]{:S(2)}, u32[]{:S(2)}) collective-permute-start(bf16[2,256,128]{2,1,0:T(8,128)(2,1)S(1)} %get-tuple-element.323), channel_id=1, source_target_pairs={{0,32},{32,64},{64,96},{96,128},{128,160},{160,192},{192,224},{224... | collective-permute-start | bytes 393224 | tf_op jit(solution)/shard_map/ppermute | solution.py:18
  207.1 14.3 %collective-permute-start.1 = (bf16[2,256,128]{2,1,0:T(8,128)(2,1)S(1)}, bf16[2,256,128]{2,1,0:T(8,128)(2,1)S(1)}, u32[]{:S(2)}, u32[]{:S(2)}) collective-permute-start(bf16[2,256,128]{2,1,0:T(8,128)(2,1)S(1)} %get-tuple-element.324), channel_id=1, source_target_pairs={{32,0},{64,32},{96,64},{128,96},{160,128},{192,160},{224,192},{256... | collective-permute-start | bytes 393224 | tf_op jit(solution)/shard_map/ppermute | solution.py:18
  280.2 5.3 copy-start.8
  281.5 48.3 %all-to-all-start.1 = ((bf16[32,128,128]{1,2,0:T(8,128)(2,1)}), bf16[32,128,128]{1,2,0:T(8,128)(2,1)S(1)}, u32[]{:S(2)}, u32[]{:S(2)}) async-start(bf16[32,128,128]{1,2,0:T(8,128)(2,1)} %copy.33), calls=%async_computation.1 | async-start | bytes 2097152 | tf_op jit(solution)/shard_map/all_to_all | solution.py:97
  285.4 47.6 %copy-start.3 = (bf16[1,128,4096]{2,1,0:T(8,128)(2,1)S(1)}, bf16[1,128,4096]{2,1,0:T(8,128)(2,1)}, u32[]{:S(2)}) copy-start(bf16[1,128,4096]{2,1,0:T(8,128)(2,1)} %param.13) | copy-start | bytes 3145732
  331.1 14.0 %collective-permute-start.2 = (bf16[128,4096]{0,1:T(8,128)(2,1)}, bf16[128,4096]{0,1:T(8,128)(2,1)S(1)}, u32[]{:S(2)}, u32[]{:S(2)}) collective-permute-start(bf16[128,4096]{0,1:T(8,128)(2,1)} %fusion.51), channel_id=1, source_target_pairs={{0,32},{32,64},{64,96},{96,128},{128,160},{160,192},{192,224},{224... | collective-permute-start | bytes 3145736 | tf_op jit(solution)/shard_map/ppermute | solution.py:18
  346.5 173.5 %all-to-all-start.2 = ((bf16[128,32,128]{0,2,1:T(8,128)(2,1)}), bf16[128,32,128]{0,2,1:T(8,128)(2,1)S(1)}, u32[]{:S(2)}, u32[]{:S(2)}) async-start(bf16[128,32,128]{0,2,1:T(8,128)(2,1)} %bitcast.24), calls=%async_computation.2 | async-start | bytes 2097152 | tf_op jit(solution)/shard_map/all_to_all | solution.py:76
  522.3 26.9 %collective-permute-start.3 = (bf16[2,256,128]{2,1,0:T(8,128)(2,1)}, bf16[2,256,128]{2,1,0:T(8,128)(2,1)S(1)}, u32[]{:S(2)}, u32[]{:S(2)}) collective-permute-start(bf16[2,256,128]{2,1,0:T(8,128)(2,1)} %get-tuple-element.319), channel_id=1, source_target_pairs={{0,32},{32,64},{64,96},{96,128},{128,160},{160,192},{192,224},{224... | collective-permute-start | bytes 393224 | tf_op jit(solution)/shard_map/ppermute | solution.py:18
  526.0 23.2 %collective-permute-start.4 = (bf16[2,256,128]{2,1,0:T(8,128)(2,1)}, bf16[2,256,128]{2,1,0:T(8,128)(2,1)S(1)}, u32[]{:S(2)}, u32[]{:S(2)}) collective-permute-start(bf16[2,256,128]{2,1,0:T(8,128)(2,1)} %get-tuple-element.320), channel_id=1, source_target_pairs={{32,0},{64,32},{96,64},{128,96},{160,128},{192,160},{224,192},{256... | collective-permute-start | bytes 393224 | tf_op jit(solution)/shard_map/ppermute | solution.py:18
  546.1 1.6 copy-start.1
  553.8 1.7 copy-start.4
  607.0 55.6 %all-to-all-start.3 = ((bf16[32,128,128]{1,2,0:T(8,128)(2,1)}), bf16[32,128,128]{1,2,0:T(8,128)(2,1)S(1)}, u32[]{:S(2)}, u32[]{:S(2)}) async-start(bf16[32,128,128]{1,2,0:T(8,128)(2,1)} %copy.37), calls=%async_computation.3 | async-start | bytes 2097152 | tf_op jit(solution)/shard_map/all_to_all | solution.py:97
where the time goes:
time: 667 us; the launch traced here: 666 us
  blocking collectives  337 us (51%)
  waiting for transfers between devices  107 us (16%)
  starting transfers between devices  72 us (11%)
  matrix products  63.7 us (10%)
  other arithmetic  35.6 us (5%)
  local copies, waits for them, and re-layouts  26 us (4%)
  loops' own time  19.9 us (3%)
    all_gather x2, blocking collectives, local(): row_scale = lax.all_gather(own_scale, 'heads', axis=0, tiled=True)  337 us
    all_to_all x2, waiting for transfers between devices, local(): lax.all_to_all(attn, 'heads', split_axis=0, concat_axis=1, tiled=True)  95.2 us
    ppermute x5, starting transfers between devices, passed_along(): return lax.ppermute(array, axis, pairs)  39.8 us
    dot_general x16, matrix products, one_group(): jnp.dot(group_q, group_k.T, preferred_element_type=jnp.float32) * scale  30.1 us
    all_to_all x2, starting transfers between devices, local(): lax.all_to_all(current, 'heads', split_axis=1, concat_axis=0, tiled=True)  24.3 us
    another operation x2, loops' own time, frame_attention(): lax.map(one_group, (query_groups, key_window, val_window, jnp.arange(grou...  19.9 us
    dot_general x16, matrix products, one_group(): result = jnp.dot(weight_local, group_v, preferred_element_type=jnp.float32)  16.3 us
  transfers between devices with their start and end apart: 9, of which 4 were waited for; matrix products, arithmetic and copies ran while one was open for 2% of the time, Pallas kernels for 0%

commit v1 on v0

v1 whole, which is shorter than its diff:
```python
import functools
import math

import jax
import jax.numpy as jnp
from jax import lax
from jax.experimental import pallas as pl
from jax.experimental.pallas import tpu as pltpu
from jax.sharding import PartitionSpec as P

FT = 256
FRAMES = 16
HALF = 128
HD = 4096
WIDTH = 128
QUEUE = 16
PLANE = 16
ROWS = 128

epsilon = 1e-06
far_below = -1e30
MESH = pl.DeviceIdType.MESH
HIGHEST = lax.Precision.HIGHEST
BF16 = jnp.bfloat16
F32 = jnp.float32


def dot_nt(a, b, precision=None):
    return lax.dot_general(
        a, b, (((1,), (1,)), ((), ())), precision=precision, preferred_element_type=F32
    )


def slot(index):
    return pl.ds(pl.multiple_of(index * FT, FT), FT)


def half_rows(index):
    return pl.ds(pl.multiple_of(index * HALF, HALF), HALF)


def columns(head):
    return pl.ds(pl.multiple_of(head * WIDTH, WIDTH), WIDTH)


def kernel(
    state, fresh, meta, q_tab, k_tab, step_tab, ref_kv,
    out,
    src, cross, fresh0, fresh0_cross,
    x0, k0, x1, k1, qs, ys, back,
    r_in, r_rows, r_full, sums, sums_other, sums_both, sums_all,
    meta_next, tables, q_scale, k_scale, step_rows, ref_k, ref_v,
    s_cross, r_cross, s_stay, r_stay, s_row, r_row, s_z, r_z, s_zrow, r_zrow,
    s_halo, r_halo, s_meta, r_meta, s_sum, r_sum, s_all, r_all,
    s_back, r_back, s_out, r_out, s_f, r_f, s_fc, r_fc, s_fz, r_fz,
):
    q = lax.axis_index("queue")
    h = lax.axis_index("heads")
    z_hi = (h // 4) % 2
    me = (h // 8) * 4 + h % 4
    other = h + 4 - 8 * z_hi
    q_next = (q + 1) % QUEUE
    q_prev = (q + QUEUE - 1) % QUEUE
    last = q == QUEUE - 1

    def head_of(place, part):
        return (place // 4) * 8 + part * 4 + place % 4

    def remote(a, b, send, recv, to_q, to_h):
        return pltpu.make_async_remote_copy(
            src_ref=a, dst_ref=b, send_sem=send, recv_sem=recv,
            device_id=(to_q, to_h), device_id_type=MESH,
        )

    def own_frame(i):
        flip = ((i // 2) + z_hi) % 2
        return i + flip * (15 - 2 * i)

    def compact(frame):
        return (frame // 4) * 2 + frame % 2

    barrier = pltpu.get_barrier_semaphore()

    def greet(to_q, to_h):
        pl.semaphore_signal(barrier, inc=1, device_id=(to_q, to_h), device_id_type=MESH)

    greet(q, other)
    greet(q_next, other)
    greet(q_prev, other)
    greet(q_next, h)
    greet(q_prev, h)

    @pl.loop(1, PLANE)
    def _(k):
        greet(q, head_of((me + k) % PLANE, z_hi))

    holds_first = jnp.logical_and(h // 8 == 0, jnp.logical_and(z_hi == 0, h % 4 < 2))
    use_fresh = jnp.logical_and(last, jnp.logical_not(holds_first))

    @pl.when(use_fresh)
    def _():
        src[...] = fresh[...]

    @pl.when(jnp.logical_not(use_fresh))
    def _():
        src[...] = state[...]

    total = jnp.zeros((HALF, WIDTH), F32)
    for block in range(HD // WIDTH):
        part = src[:, block * WIDTH : (block + 1) * WIDTH].astype(F32)
        total = total + part * part
    ones = jnp.ones((8, WIDTH), F32)
    own_row = lax.rsqrt(dot_nt(ones, total, HIGHEST) / HD + epsilon)

    def modulation(sweep, table_of):
        levels = table_of[0:FRAMES, :]
        lanes = lax.broadcasted_iota(jnp.int32, (FRAMES, 128), 1)
        one_hot = (levels == lanes).astype(F32)
        for table, result in ((0, q_scale), (1, k_scale)):
            result[sweep] = lax.dot_general(
                one_hot, tables[table], (((1,), (0,)), ((), ())),
                precision=HIGHEST, preferred_element_type=F32,
            )
        picked = jnp.sum(one_hot * step_tab[...], axis=1, keepdims=True)
        step_rows[sweep] = jnp.broadcast_to(picked, (FRAMES, WIDTH))
        wanted = table_of[FRAMES : FRAMES + 1, :]
        for part, result in ((0, ref_k), (1, ref_v)):
            chosen = jnp.zeros((FT, WIDTH), F32)
            for request in range(ref_kv.shape[1]):
                chosen = jnp.where(wanted == request, ref_kv[part, request].astype(F32), chosen)
            result[sweep] = chosen.astype(BF16)

    tables[...] = jnp.zeros_like(tables)
    tables[0, 0:48, :] = q_tab[...]
    tables[1, 0:48, :] = k_tab[...]
    modulation(0, meta.at[0])

    r_in[me] = own_row
    pl.semaphore_wait(barrier, PLANE - 1 + 5)

    def row_copy(place):
        return remote(r_in.at[me], r_in.at[me], s_row.at[place], r_row.at[me], q, head_of(place, z_hi))

    def cross_copy(place):
        return remote(
            src.at[:, columns(head_of(place, 1 - z_hi))], cross.at[half_rows(me)],
            s_cross.at[place], r_cross.at[me], q, head_of(place, z_hi),
        )

    def stay_rows(place):
        return half_rows(2 + (place // 4) * 8 + z_hi * 4 + place % 4)

    def stay_copy(place):
        return remote(
            src.at[:, columns(head_of(place, z_hi))], x0.at[stay_rows(me)],
            s_stay.at[place], r_stay.at[me], q, head_of(place, z_hi),
        )

    @pl.loop(1, PLANE)
    def _(k):
        row_copy((me + k) % PLANE).start()

    own_cross = pltpu.make_async_copy(
        src.at[:, columns(other)], cross.at[half_rows(me)], r_cross.at[me]
    )
    own_cross.start()

    @pl.loop(1, PLANE)
    def _(k):
        cross_copy((me + k) % PLANE).start()

    own_stay = pltpu.make_async_copy(src.at[:, columns(h)], x0.at[stay_rows(me)], r_stay.at[me])
    own_stay.start()

    @pl.loop(1, PLANE)
    def _(k):
        stay_copy((me + k) % PLANE).start()

    meta_copy = remote(meta.at[1], meta_next, s_meta, r_meta, q_prev, h)
    meta_copy.start()

    def fresh0_copy(place, crossing):
        half = h % 4
        part = z_hi + crossing * (1 - 2 * z_hi)
        target = fresh0_cross if crossing else fresh0
        send, recv = (s_fc, r_fc) if crossing else (s_f, r_f)
        return remote(
            fresh.at[:, columns(head_of(place, part))], target.at[half_rows(half)],
            send.at[place], recv.at[half], q, head_of(place, z_hi),
        )

    gives_fresh0 = jnp.logical_and(last, holds_first)

    @pl.when(gives_fresh0)
    def _():
        half = h % 4
        pltpu.make_async_copy(
            fresh.at[:, columns(other)], fresh0_cross.at[half_rows(half)], r_fc.at[half]
        ).start()
        pltpu.make_async_copy(
            fresh.at[:, columns(h)], fresh0.at[half_rows(half)], r_f.at[half]
        ).start()

        @pl.loop(1, PLANE)
        def _(k):
            fresh0_copy((me + k) % PLANE, 1).start()
            fresh0_copy((me + k) % PLANE, 0).start()

    def wait_bytes(ref, sem):
        pltpu.make_async_copy(ref, ref, sem).wait()

    @pl.loop(1, PLANE)
    def _(k):
        place = (me + k) % PLANE
        wait_bytes(r_in.at[place], r_row.at[place])

    for place in range(PLANE):
        r_rows[z_hi, place : place + 1, :] = r_in[place, 0:1, :]
    zrow_copy = remote(r_rows.at[z_hi], r_rows.at[z_hi], s_zrow, r_zrow, q, other)
    zrow_copy.start()

    def z_copy(i):
        frame = own_frame(i)
        return remote(
            cross.at[slot(compact(frame))], x0.at[slot(frame + 1)], s_z.at[i], r_z.at[i], q, other
        )

    def send_z(i):
        c = compact(own_frame(i))
        wait_bytes(cross.at[half_rows(2 * c)], r_cross.at[2 * c])
        wait_bytes(cross.at[half_rows(2 * c + 1)], r_cross.at[2 * c + 1])
        z_copy(i).start()

    @pl.loop(0, 2)
    def _(i):
        send_z(i)

    fresh0_z = remote(fresh0_cross, fresh0, s_fz, r_fz, q, other)
    relays_fresh0 = jnp.logical_and(last, z_hi == 0)
    takes_fresh0 = jnp.logical_and(last, z_hi == 1)

    @pl.when(relays_fresh0)
    def _():
        for half in range(2):
            wait_bytes(fresh0_cross.at[half_rows(half)], r_fc.at[half])
        fresh0_z.start()

    @pl.loop(2, 8)
    def _(i):
        send_z(i)

    def spread(rows_value, count, target_rows):
        padded = jnp.concatenate(
            [rows_value, jnp.zeros((128 - rows_value.shape[0], 128), F32)], axis=0
        )
        turned = jnp.transpose(padded)
        for index in range(count):
            r_full[target_rows(index), :] = jnp.broadcast_to(turned[:, index : index + 1], (128, 128))

    wait_bytes(r_rows.at[1 - z_hi], r_zrow)

    def first_rows(index):
        part, place = index // PLANE, index % PLANE
        chunk = (place // 4) * 8 + part * 4 + place % 4
        return half_rows(chunk)

    spread(jnp.concatenate([r_rows[0], r_rows[1]], axis=0), 2 * PLANE, first_rows)

    def prepare(sweep, x_ref, k_ref, frame):
        normed = x_ref[slot(frame + 1), :].astype(F32) * r_full[slot(frame), :]
        qs[slot(frame), :] = (normed * q_scale[sweep, pl.ds(frame, 1), :]).astype(BF16)
        k_ref[slot(frame + 1), :] = (normed * k_scale[sweep, pl.ds(frame, 1), :]).astype(BF16)

    factor = math.log2(math.e) / math.sqrt(WIDTH)

    def attend(sweep, x_ref, k_ref, frame, no_prev, no_next, target, target_slot):
        before = jnp.where(jnp.logical_and(frame == 0, no_prev), far_below, 0.0).astype(F32)
        after = jnp.where(jnp.logical_and(frame == FRAMES - 1, no_next), far_below, 0.0).astype(F32)
        step = step_rows[sweep, pl.ds(frame, 1), :]

        @pl.loop(0, FT // ROWS)
        def _(chunk):
            start = pl.multiple_of(frame * FT + chunk * ROWS, ROWS)
            query = qs[pl.ds(start, ROWS), :]
            scores = []
            for part in range(3):
                scores.append(dot_nt(query, k_ref[slot(frame + part), :]))
            scores[0] = scores[0] + before
            scores[2] = scores[2] + after
            scores.append(dot_nt(query, ref_k[sweep]))
            high = jnp.maximum(
                jnp.maximum(scores[0], scores[1]), jnp.maximum(scores[2], scores[3])
            )
            high = jnp.max(high, axis=1, keepdims=True)
            probs = [jnp.exp2((part - high) * factor) for part in scores]
            weight = (probs[0] + probs[1]) + (probs[2] + probs[3])
            weight = jnp.sum(weight, axis=1, keepdims=True)
            result = jnp.dot(probs[3].astype(BF16), ref_v[sweep], preferred_element_type=F32)
            for part in range(3):
                result = result + jnp.dot(
                    probs[part].astype(BF16), x_ref[slot(frame + part), :],
                    preferred_element_type=F32,
                )
            attn = (result / weight).astype(BF16).astype(F32)
            held = x_ref[pl.ds(start + FT, ROWS), :].astype(F32)
            place = pl.multiple_of(target_slot * FT + chunk * ROWS, ROWS)
            target[pl.ds(place, ROWS), :] = (held + step * attn).astype(BF16)

    def halo_copies(sweep, x_ref, k_ref):
        copies = []
        for index, (ref, here, there, to_q) in enumerate((
            (k_ref, 1, 17, q_prev), (x_ref, 1, 17, q_prev),
            (k_ref, 16, 0, q_next), (x_ref, 16, 0, q_next),
        )):
            copies.append(remote(
                ref.at[slot(here)], ref.at[slot(there)],
                s_halo.at[sweep, index], r_halo.at[sweep, index], to_q, h,
            ))
        return copies

    def start_halo(sweep, x_ref, k_ref):
        for copy in halo_copies(sweep, x_ref, k_ref):
            copy.start()

    def wait_halo(sweep, x_ref, k_ref):
        for copy in halo_copies(sweep, x_ref, k_ref):
            copy.wait_recv()

    def arrive(i):
        frame = own_frame(i)
        c = compact(frame)
        for half in range(2):
            wait_bytes(x0.at[half_rows(2 * (frame + 1) + half)], r_stay.at[2 * c + half])
        wait_bytes(x0.at[slot(16 - frame)], r_z.at[i])

    def first_pairs(i0, count):
        @pl.loop(0, 2 * count)
        def _(k):
            i = i0 + k // 2
            frame = i + (k % 2) * (15 - 2 * i)
            attend(0, x0, k0, frame, q == 0, last, x1, frame + 1)

            @pl.when(last)
            def _():
                x1[slot(frame + 1), :] = x0[slot(frame + 1), :]

    def take_fresh0():
        @pl.when(jnp.logical_and(last, z_hi == 0))
        def _():
            for half in range(2):
                wait_bytes(fresh0.at[half_rows(half)], r_f.at[half])

        @pl.when(takes_fresh0)
        def _():
            wait_bytes(fresh0, r_fz)

        @pl.when(last)
        def _():
            x1[slot(1), :] = fresh0[...]

    def sum_copy(group):
        return remote(
            sums.at[group], sums_other.at[group], s_sum.at[group], r_sum.at[group], q, other
        )

    def start_sums(group):
        for index in range(4):
            i = 2 * group + index // 2
            frame = i if index % 2 == 0 else 15 - i
            held = x1[slot(frame + 1), :].astype(F32)
            row = dot_nt(ones, held * held, HIGHEST)
            sums[group, 2 * index : 2 * index + 1, :] = row[0:1, 0:128]
            sums[group, 2 * index + 1 : 2 * index + 2, :] = row[0:1, 128:256]
        sum_copy(group).start()

    def all_copy(group, place):
        return remote(
            sums_both.at[group], sums_all.at[group, me],
            s_all.at[group, place], r_all.at[group, me], q, head_of(place, z_hi),
        )

    def spread_sums(group):
        wait_bytes(sums_other.at[group], r_sum.at[group])
        both = sums[group] + sums_other[group]
        sums_both[group] = both

        @pl.loop(1, PLANE)
        def _(k):
            all_copy(group, (me + k) % PLANE).start()

        sums_all[group, me] = both

    def prepare_group(group):
        @pl.loop(1, PLANE)
        def _(k):
            place = (me + k) % PLANE
            wait_bytes(sums_all.at[group, place], r_all.at[group, place])

        whole = sums_all[group, 0]
        for place in range(1, PLANE):
            whole = whole + sums_all[group, place]
        rows = lax.rsqrt(whole / HD + epsilon)

        def group_rows(index):
            i = 2 * group + index // 4
            frame = i if (index // 2) % 2 == 0 else 15 - i
            return half_rows(2 * frame + index % 2)

        spread(rows, 8, group_rows)

        @pl.loop(0, 4)
        def _(k):
            i = 2 * group + k // 2
            prepare(1, x1, k1, i + (k % 2) * (15 - 2 * i))

    def back_copy(frame):
        moves = ((frame // 2) + z_hi) % 2
        return remote(
            ys.at[slot(frame)], back.at[moves, slot(compact(frame))],
            s_back.at[frame], r_back.at[moves, compact(frame)],
            q_next, h + moves * (4 - 8 * z_hi),
        )

    def second_pairs(i0, count):
        @pl.loop(0, 2 * count)
        def _(k):
            i = i0 + k // 2
            frame = i + (k % 2) * (15 - 2 * i)
            attend(1, x1, k1, frame, last, q == QUEUE - 2, ys, frame)
            back_copy(frame).start()

    def prepare_pair(i):
        @pl.loop(0, 2)
        def _(k):
            prepare(0, x0, k0, i + k * (15 - 2 * i))

    arrive(0)
    prepare_pair(0)
    start_halo(0, x0, k0)
    arrive(1)
    prepare_pair(1)
    wait_halo(0, x0, k0)
    first_pairs(0, 1)
    take_fresh0()
    arrive(2)
    prepare_pair(2)
    first_pairs(1, 1)
    start_sums(0)
    wait_bytes(meta_next, r_meta)
    modulation(1, meta_next)
    arrive(3)
    prepare_pair(3)
    first_pairs(2, 1)
    spread_sums(0)
    arrive(4)
    prepare_pair(4)
    first_pairs(3, 1)
    start_sums(1)
    arrive(5)
    prepare_pair(5)
    first_pairs(4, 1)
    spread_sums(1)
    arrive(6)
    prepare_pair(6)
    first_pairs(5, 1)
    start_sums(2)
    arrive(7)
    prepare_pair(7)
    first_pairs(6, 2)
    start_sums(3)
    prepare_group(0)
    start_halo(1, x1, k1)
    prepare_group(1)
    wait_halo(1, x1, k1)
    second_pairs(0, 1)
    second_pairs(1, 2)
    spread_sums(2)
    prepare_group(2)
    second_pairs(3, 2)
    spread_sums(3)
    prepare_group(3)
    second_pairs(5, 3)

    def out_copy(part, c, half):
        place = 2 * c + half
        head = h + part * (4 - 8 * z_hi)
        return remote(
            back.at[part, half_rows(place)], out.at[:, columns(head)],
            s_out.at[part, place], r_out.at[part, me], q, head_of(place, z_hi),
        )

    def out_local(part):
        head = h + part * (4 - 8 * z_hi)
        return pltpu.make_async_copy(
            back.at[part, half_rows(me)], out.at[:, columns(head)], r_out.at[part, me]
        )

    @pl.loop(0, 16)
    def _(k):
        c = compact(own_frame(k // 2))
        part = k % 2
        wait_bytes(back.at[part, slot(c)], r_back.at[part, c])
        for half in range(2):
            place = 2 * c + half

            @pl.when(place == me)
            def _():
                out_local(part).start()

            @pl.when(place != me)
            def _():
                out_copy(part, c, half).start()

    @pl.loop(0, 2 * PLANE)
    def _(k):
        part, place = k // PLANE, k % PLANE
        head = head_of(place, z_hi + part - 2 * z_hi * part)
        wait_bytes(out.at[:, columns(head)], r_out.at[part, place])

    @pl.loop(1, PLANE)
    def _(k):
        place = (me + k) % PLANE
        row_copy(place).wait_send()
        cross_copy(place).wait_send()
        stay_copy(place).wait_send()
        for part in range(2):
            out_copy(part, place // 2, place % 2).wait_send()
        for group in range(4):
            all_copy(group, place).wait_send()

    @pl.when(gives_fresh0)
    def _():
        @pl.loop(1, PLANE)
        def _(k):
            fresh0_copy((me + k) % PLANE, 1).wait_send()
            fresh0_copy((me + k) % PLANE, 0).wait_send()

    @pl.when(relays_fresh0)
    def _():
        fresh0_z.wait_send()

    meta_copy.wait_send()
    zrow_copy.wait_send()

    @pl.loop(0, 8)
    def _(i):
        z_copy(i).wait_send()

    for group in range(4):
        sum_copy(group).wait_send()
    for sweep, (x_ref, k_ref) in enumerate(((x0, k0), (x1, k1))):
        for copy in halo_copies(sweep, x_ref, k_ref):
            copy.wait_send()

    @pl.loop(0, FRAMES)
    def _(frame):
        back_copy(frame).wait_send()


def local(state, fresh, frame_level, request, q_table, k_table, step_size, reference_kv):
    meta = jnp.concatenate(
        [
            jnp.broadcast_to(frame_level[:, :, None], (2, FRAMES, 128)),
            jnp.broadcast_to(request[:, :, None], (2, 8, 128)),
        ],
        axis=1,
    )
    step_tab = jnp.pad(step_size, (0, 128 - step_size.shape[0]))[None, :]
    block = FRAMES * FT
    dma = pltpu.SemaphoreType.DMA
    vmem = pl.BlockSpec(memory_space=pltpu.VMEM)
    return pl.pallas_call(
        kernel,
        out_shape=jax.ShapeDtypeStruct(state.shape, state.dtype),
        in_specs=[vmem] * 7,
        out_specs=vmem,
        scratch_shapes=[
            pltpu.VMEM((HALF, HD), BF16),
            pltpu.VMEM((block // 2, WIDTH), BF16),
            pltpu.VMEM((FT, WIDTH), BF16),
            pltpu.VMEM((FT, WIDTH), BF16),
            pltpu.VMEM((block + 2 * FT, WIDTH), BF16),
            pltpu.VMEM((block + 2 * FT, WIDTH), BF16),
            pltpu.VMEM((block + 2 * FT, WIDTH), BF16),
            pltpu.VMEM((block + 2 * FT, WIDTH), BF16),
            pltpu.VMEM((block, WIDTH), BF16),
            pltpu.VMEM((block, WIDTH), BF16),
            pltpu.VMEM((2, block // 2, WIDTH), BF16),
            pltpu.VMEM((PLANE, 8, 128), F32),
            pltpu.VMEM((2, PLANE, 128), F32),
            pltpu.VMEM((block, 128), F32),
            pltpu.VMEM((4, 8, 128), F32),
            pltpu.VMEM((4, 8, 128), F32),
            pltpu.VMEM((4, 8, 128), F32),
            pltpu.VMEM((4, PLANE, 8, 128), F32),
            pltpu.VMEM((24, 128), jnp.int32),
            pltpu.VMEM((2, 128, WIDTH), F32),
            pltpu.VMEM((2, FRAMES, WIDTH), F32),
            pltpu.VMEM((2, FRAMES, WIDTH), F32),
            pltpu.VMEM((2, FRAMES, WIDTH), F32),
            pltpu.VMEM((2, FT, WIDTH), BF16),
            pltpu.VMEM((2, FT, WIDTH), BF16),
            dma((PLANE,)), dma((PLANE,)), dma((PLANE,)), dma((PLANE,)), dma((PLANE,)), dma((PLANE,)),
            dma((8,)), dma((8,)), dma, dma,
            dma((2, 4)), dma((2, 4)), dma, dma, dma((4,)), dma((4,)), dma((4, PLANE)), dma((4, PLANE)),
            dma((FRAMES,)), dma((2, 8)), dma((2, PLANE)), dma((2, PLANE)),
            dma((PLANE,)), dma((2,)), dma((PLANE,)), dma((2,)), dma, dma,
        ],
        compiler_params=pltpu.CompilerParams(
            collective_id=0, has_side_effects=True, vmem_limit_bytes=48 << 20
        ),
    )(state, fresh[0], meta, q_table, k_table, step_tab, reference_kv)


def solution(mesh):
    placed = (
        P(("queue", "heads"), None),
        P(None, "heads", None),
        P(None, "queue"),
        P(None, "queue"),
        P(None, "heads"),
        P(None, "heads"),
        P(),
        P(None, None, None, "heads"),
    )
    return jax.shard_map(
        local, mesh=mesh, in_specs=placed, out_specs=P(("queue", "heads"), None), check_vma=False
    )
```

time: 667 us -> 208 us (0.31)
  the two profiles are of different devices: /device:TPU:33 before, /device:TPU:132 now
where the time goes in v1:
time: 208 us; the launch traced here: 207 us
  Pallas kernels  200 us (96%)
  local copies, waits for them, and re-layouts  7.27 us (3%)
    pallas_call x1, Pallas kernels, local(): pl.pallas_call(kernel, out_shape=jax.ShapeDtypeStruct(state.shape, state....  200 us
    unnamed x17, local copies, waits for them, and re-layouts  7.13 us

profile of v1, /device:TPU:132, one launch (start us, length us, event | category | flops | bytes accessed | tf_op | source)
XLA Modules:
  0.0 207.3 jit_solution(11676605253901274602)
XLA Ops:
  0.0 0.0 copy-start.7
  0.0 0.7 copy-done.7
  0.7 0.0 copy-start.6
  0.7 0.6 copy-done.6
  1.3 0.0 copy-start.5
  1.3 0.1 broadcast_in_dim.19
  1.4 0.6 copy-done.5
  2.0 0.1 broadcast_in_dim.8
  2.1 0.0 copy-start.3
  2.1 0.0 copy-start.4
  2.1 0.7 copy-done.3
  2.8 0.0 copy-done.4
  2.8 0.0 copy-start
  2.8 1.2 copy-done
  4.0 0.0 copy-start.1
  4.0 1.2 copy-done.1
  5.3 0.0 copy-start.2
  5.3 1.0 copy-done.2
  6.3 200.0 %shard_map.82 = bf16[128,4096]{1,0:T(8,128)(2,1)S(1)} custom-call(bf16[128,4096]{1,0:T(8,128)(2,1)S(1)} %copy-done, bf16[128,4096]{1,0:T(8,128)(2,1)S(1)} %bitcast.4, s32[2,24,128]{2,1,0:T(8,128)S(1)} %pad_add_fusion.meta, f32[48,128]{1,0:T(8,128)S(1)} %copy-done.3, f32[48,128]{1,0:T(8,128)S(1)} %copy-done.4, f32[1,128]{1,0:T(1,128)S(1)} %pad_bitcast_fusion.step_tab, ...), custom_call_target="tpu_custom_call" | custom-call | tf_op jit(solution)/shard_map/pallas_call | solution.py:572
  206.3 1.0 copy.10
  (2 shorter events, 0.0 us)
Async XLA Ops:
  0.0 0.7 copy-start.7
  0.7 0.7 copy-start.6
  1.3 0.7 copy-start.5
  2.1 0.7 copy-start.3
  2.1 0.8 copy-start.4
  2.8 1.2 copy-start
  4.0 1.2 copy-start.1
  5.3 1.0 copy-start.2

commit v2 on v1

--- a/solution.py
+++ b/solution.py
@@ -15,7 +15,8 @@
 WIDTH = 128
 QUEUE = 16
 PLANE = 16
-ROWS = 128
+ROWS = 256
+RELAYED = 6
 
 epsilon = 1e-06
 far_below = -1e30
@@ -44,15 +45,17 @@
 
 
 def kernel(
-    state, fresh, meta, q_tab, k_tab, step_tab, ref_kv,
+    state, fresh, frame_level, request, q_tab, k_tab, step_size, ref_in,
     out,
     src, cross, fresh0, fresh0_cross,
     x0, k0, x1, k1, qs, ys, back,
     r_in, r_rows, r_full, sums, sums_other, sums_both, sums_all,
-    meta_next, tables, q_scale, k_scale, step_rows, ref_k, ref_v,
+    levels, levels_next, wanted, wanted_next, tables, step_tab, ref_kv, level_pad,
+    q_scale, k_scale, step_rows, ref_k, ref_v,
     s_cross, r_cross, s_stay, r_stay, s_row, r_row, s_z, r_z, s_zrow, r_zrow,
     s_halo, r_halo, s_meta, r_meta, s_sum, r_sum, s_all, r_all,
     s_back, r_back, s_out, r_out, s_f, r_f, s_fc, r_fc, s_fz, r_fz,
+    load, via, s_via, r_via,
 ):
     q = lax.axis_index("queue")
     h = lax.axis_index("heads")
@@ -90,6 +93,18 @@
     greet(q_next, h)
     greet(q_prev, h)
 
+    relays_fresh0 = jnp.logical_and(q == 1, z_hi == 0)
+    takes_fresh0 = jnp.logical_and(last, z_hi == 1)
+
+    @pl.when(relays_fresh0)
+    def _():
+        greet(QUEUE - 1, other)
+
+    @pl.when(takes_fresh0)
+    def _():
+        greet(1, other)
+
+
     @pl.loop(1, PLANE)
     def _(k):
         greet(q, head_of((me + k) % PLANE, z_hi))
@@ -99,11 +114,23 @@
 
     @pl.when(use_fresh)
     def _():
-        src[...] = fresh[...]
+        pltpu.make_async_copy(fresh, src, load.at[0]).start()
 
     @pl.when(jnp.logical_not(use_fresh))
     def _():
-        src[...] = state[...]
+        pltpu.make_async_copy(state, src, load.at[0]).start()
+
+    tables[...] = jnp.zeros_like(tables)
+    loads = [
+        pltpu.make_async_copy(a, b, load.at[1 + index])
+        for index, (a, b) in enumerate((
+            (frame_level, levels), (request, wanted), (step_size, step_tab),
+            (q_tab, tables.at[0, 0:48]), (k_tab, tables.at[1, 0:48]), (ref_in, ref_kv),
+        ))
+    ]
+    for copy in loads:
+        copy.start()
+    pltpu.make_async_copy(state, src, load.at[0]).wait()
 
     total = jnp.zeros((HALF, WIDTH), F32)
     for block in range(HD // WIDTH):
@@ -112,31 +139,34 @@
     ones = jnp.ones((8, WIDTH), F32)
     own_row = lax.rsqrt(dot_nt(ones, total, HIGHEST) / HD + epsilon)
 
-    def modulation(sweep, table_of):
-        levels = table_of[0:FRAMES, :]
-        lanes = lax.broadcasted_iota(jnp.int32, (FRAMES, 128), 1)
-        one_hot = (levels == lanes).astype(F32)
+    def modulation(sweep, level_ref, wanted_ref):
+        level_pad[...] = jnp.zeros_like(level_pad)
+        level_pad[0:2, 0:FRAMES] = level_ref[...].astype(F32)
+        turned = jnp.transpose(level_pad[...])
+        own = turned[0:FRAMES, sweep : sweep + 1]
+        lanes = lax.broadcasted_iota(jnp.int32, (FRAMES, 128), 1).astype(F32)
+        one_hot = (jnp.broadcast_to(own, (FRAMES, 128)) == lanes).astype(F32)
         for table, result in ((0, q_scale), (1, k_scale)):
             result[sweep] = lax.dot_general(
                 one_hot, tables[table], (((1,), (0,)), ((), ())),
                 precision=HIGHEST, preferred_element_type=F32,
             )
-        picked = jnp.sum(one_hot * step_tab[...], axis=1, keepdims=True)
+        picked = jnp.sum(one_hot[:, 0:48] * step_tab[...], axis=1, keepdims=True)
         step_rows[sweep] = jnp.broadcast_to(picked, (FRAMES, WIDTH))
-        wanted = table_of[FRAMES : FRAMES + 1, :]
+        choice = jnp.broadcast_to(wanted_ref[sweep : sweep + 1, :], (FT, WIDTH))
         for part, result in ((0, ref_k), (1, ref_v)):
             chosen = jnp.zeros((FT, WIDTH), F32)
-            for request in range(ref_kv.shape[1]):
-                chosen = jnp.where(wanted == request, ref_kv[part, request].astype(F32), chosen)
+            for index in range(ref_kv.shape[1]):
+                chosen = jnp.where(choice == index, ref_kv[part, index].astype(F32), chosen)
             result[sweep] = chosen.astype(BF16)
 
-    tables[...] = jnp.zeros_like(tables)
-    tables[0, 0:48, :] = q_tab[...]
-    tables[1, 0:48, :] = k_tab[...]
-    modulation(0, meta.at[0])
+    for copy in loads:
+        copy.wait()
+    modulation(0, levels, wanted)
 
     r_in[me] = own_row
-    pl.semaphore_wait(barrier, PLANE - 1 + 5)
+    extra = jnp.logical_or(relays_fresh0, takes_fresh0).astype(jnp.int32)
+    pl.semaphore_wait(barrier, PLANE - 1 + 5 + extra)
 
     def row_copy(place):
         return remote(r_in.at[me], r_in.at[me], s_row.at[place], r_row.at[me], q, head_of(place, z_hi))
@@ -176,8 +206,12 @@
     def _(k):
         stay_copy((me + k) % PLANE).start()
 
-    meta_copy = remote(meta.at[1], meta_next, s_meta, r_meta, q_prev, h)
-    meta_copy.start()
+    meta_copies = [
+        remote(levels, levels_next, s_meta.at[0], r_meta.at[0], q_prev, h),
+        remote(wanted, wanted_next, s_meta.at[1], r_meta.at[1], q_prev, h),
+    ]
+    for copy in meta_copies:
+        copy.start()
 
     def fresh0_copy(place, crossing):
         half = h % 4
@@ -190,21 +224,21 @@
         )
 
     gives_fresh0 = jnp.logical_and(last, holds_first)
-
-    @pl.when(gives_fresh0)
-    def _():
-        half = h % 4
-        pltpu.make_async_copy(
-            fresh.at[:, columns(other)], fresh0_cross.at[half_rows(half)], r_fc.at[half]
-        ).start()
-        pltpu.make_async_copy(
-            fresh.at[:, columns(h)], fresh0.at[half_rows(half)], r_f.at[half]
-        ).start()
-
-        @pl.loop(1, PLANE)
-        def _(k):
-            fresh0_copy((me + k) % PLANE, 1).start()
-            fresh0_copy((me + k) % PLANE, 0).start()
+    gives_cross0 = jnp.logical_and(q == 1, holds_first)
+
+    for gives, crossing, head, target, recv in (
+        (gives_cross0, 1, other, fresh0_cross, r_fc), (gives_fresh0, 0, h, fresh0, r_f),
+    ):
+        @pl.when(gives)
+        def _():
+            half = h % 4
+            pltpu.make_async_copy(
+                fresh.at[:, columns(head)], target.at[half_rows(half)], recv.at[half]
+            ).start()
+
+            @pl.loop(1, PLANE)
+            def _(k):
+                fresh0_copy((me + k) % PLANE, crossing).start()
 
     def wait_bytes(ref, sem):
         pltpu.make_async_copy(ref, ref, sem).wait()
@@ -231,23 +265,18 @@
         wait_bytes(cross.at[half_rows(2 * c + 1)], r_cross.at[2 * c + 1])
         z_copy(i).start()
 
-    @pl.loop(0, 2)
-    def _(i):
-        send_z(i)
-
-    fresh0_z = remote(fresh0_cross, fresh0, s_fz, r_fz, q, other)
-    relays_fresh0 = jnp.logical_and(last, z_hi == 0)
-    takes_fresh0 = jnp.logical_and(last, z_hi == 1)
-
-    @pl.when(relays_fresh0)
-    def _():
-        for half in range(2):
-            wait_bytes(fresh0_cross.at[half_rows(half)], r_fc.at[half])
-        fresh0_z.start()
-
-    @pl.loop(2, 8)
-    def _(i):
-        send_z(i)
+    fresh0_z = remote(fresh0_cross, fresh0, s_fz, r_fz, QUEUE - 1, other)
+
+    def send_fresh0():
+        @pl.when(relays_fresh0)
+        def _():
+            for half in range(2):
+                wait_bytes(fresh0_cross.at[half_rows(half)], r_fc.at[half])
+            fresh0_z.start()
+
+    send_z(0)
+    send_z(1)
+    send_fresh0()
 
     def spread(rows_value, count, target_rows):
         padded = jnp.concatenate(
@@ -318,13 +347,42 @@
             ))
         return copies
 
+    def halo_roles(sweep):
+        if sweep == 0:
+            return q != 0, q < QUEUE - 2, q != QUEUE - 1, jnp.logical_and(q != 0, q != QUEUE - 1)
+        return q != QUEUE - 1, q != QUEUE - 2, q != QUEUE - 2, q != QUEUE - 1
+
     def start_halo(sweep, x_ref, k_ref):
-        for copy in halo_copies(sweep, x_ref, k_ref):
-            copy.start()
+        copies = halo_copies(sweep, x_ref, k_ref)
+        to_prev, to_next, from_next, from_prev = halo_roles(sweep)
+        for group, wanted_here in ((copies[:2], to_prev), (copies[2:], to_next)):
+            @pl.when(wanted_here)
+            def _():
+                for copy in group:
+                    copy.start()
+        for rim, absent in ((17, jnp.logical_not(from_next)), (0, jnp.logical_not(from_prev))):
+            @pl.when(absent)
+            def _():
+                for ref in (x_ref, k_ref):
+                    ref[slot(rim), :] = jnp.zeros((FT, WIDTH), BF16)
 
     def wait_halo(sweep, x_ref, k_ref):
-        for copy in halo_copies(sweep, x_ref, k_ref):
-            copy.wait_recv()
+        copies = halo_copies(sweep, x_ref, k_ref)
+        _, _, from_next, from_prev = halo_roles(sweep)
+        for group, wanted_here in ((copies[:2], from_next), (copies[2:], from_prev)):
+            @pl.when(wanted_here)
+            def _():
+                for copy in group:
+                    copy.wait_recv()
+
+    def wait_halo_sent(sweep, x_ref, k_ref):
+        copies = halo_copies(sweep, x_ref, k_ref)
+        to_prev, to_next, _, _ = halo_roles(sweep)
+        for group, wanted_here in ((copies[:2], to_prev), (copies[2:], to_next)):
+            @pl.when(wanted_here)
+            def _():
+                for copy in group:
+                    copy.wait_send()
 
     def arrive(i):
         frame = own_frame(i)
@@ -338,7 +396,10 @@
         def _(k):
             i = i0 + k // 2
             frame = i + (k % 2) * (15 - 2 * i)
-            attend(0, x0, k0, frame, q == 0, last, x1, frame + 1)
+
+            @pl.when(jnp.logical_not(last))
+            def _():
+                attend(0, x0, k0, frame, q == 0, last, x1, frame + 1)
 
             @pl.when(last)
             def _():
@@ -421,65 +482,114 @@
             q_next, h + moves * (4 - 8 * z_hi),
         )
 
+    def is_relayed(i, frame):
+        moves = ((frame // 2) + z_hi) % 2
+        far = jnp.where(last, 0, 1)
+        return jnp.logical_and(q % 4 == 3, jnp.logical_and(moves == far, i < RELAYED))
+
+    def via_copy(i, frame):
+        near = h + jnp.where(last, 1, 0) * (4 - 8 * z_hi)
+        return remote(
+            ys.at[slot(frame)], via.at[slot(i)], s_back.at[frame], r_via.at[i], q_next, near
+        )
+
+    def onward_copy(i):
+        c = compact(15 - own_frame(i))
+        part = jnp.where(q == 0, 0, 1)
+        return remote(
+            via.at[slot(i)], back.at[part, slot(c)], s_via.at[i], r_back.at[part, c], q, other
+        )
+
+    def relay_back(i):
+        @pl.when(q % 4 == 0)
+        def _():
+            wait_bytes(via.at[slot(i)], r_via.at[i])
+            onward_copy(i).start()
+
     def second_pairs(i0, count):
         @pl.loop(0, 2 * count)
         def _(k):
             i = i0 + k // 2
             frame = i + (k % 2) * (15 - 2 * i)
             attend(1, x1, k1, frame, last, q == QUEUE - 2, ys, frame)
-            back_copy(frame).start()
+
+            @pl.when(is_relayed(i, frame))
+            def _():
+                via_copy(i, frame).start()
+
+            @pl.when(jnp.logical_not(is_relayed(i, frame)))
+            def _():
+                back_copy(frame).start()
 
     def prepare_pair(i):
         @pl.loop(0, 2)
         def _(k):
             prepare(0, x0, k0, i + k * (15 - 2 * i))
 
+    def next_z(i):
+        z_copy(i - 2).wait_send()
+        send_z(i)
+
+    next_z(2)
     arrive(0)
     prepare_pair(0)
     start_halo(0, x0, k0)
+    next_z(3)
     arrive(1)
     prepare_pair(1)
     wait_halo(0, x0, k0)
     first_pairs(0, 1)
-    take_fresh0()
+    next_z(4)
     arrive(2)
     prepare_pair(2)
     first_pairs(1, 1)
-    start_sums(0)
-    wait_bytes(meta_next, r_meta)
-    modulation(1, meta_next)
+    next_z(5)
     arrive(3)
     prepare_pair(3)
     first_pairs(2, 1)
-    spread_sums(0)
+    for index in range(2):
+        meta_copies[index].wait_recv()
+    modulation(1, levels_next, wanted_next)
+    next_z(6)
+    take_fresh0()
+    start_sums(0)
     arrive(4)
     prepare_pair(4)
     first_pairs(3, 1)
     start_sums(1)
+    next_z(7)
+    spread_sums(0)
     arrive(5)
     prepare_pair(5)
     first_pairs(4, 1)
     spread_sums(1)
+    prepare_group(0)
+    start_halo(1, x1, k1)
     arrive(6)
     prepare_pair(6)
     first_pairs(5, 1)
     start_sums(2)
+    wait_halo(1, x1, k1)
+    second_pairs(0, 1)
     arrive(7)
     prepare_pair(7)
     first_pairs(6, 2)
     start_sums(3)
-    prepare_group(0)
-    start_halo(1, x1, k1)
     prepare_group(1)
-    wait_halo(1, x1, k1)
-    second_pairs(0, 1)
-    second_pairs(1, 2)
+    second_pairs(1, 1)
     spread_sums(2)
+    relay_back(0)
+    second_pairs(2, 1)
+    spread_sums(3)
+    relay_back(1)
     prepare_group(2)
     second_pairs(3, 2)
-    spread_sums(3)
+    relay_back(2)
     prepare_group(3)
     second_pairs(5, 3)
+    relay_back(3)
+    relay_back(4)
+    relay_back(5)
 
     def out_copy(part, c, half):
         place = 2 * c + half
@@ -528,51 +638,47 @@
         for group in range(4):
             all_copy(group, place).wait_send()
 
-    @pl.when(gives_fresh0)
-    def _():
-        @pl.loop(1, PLANE)
-        def _(k):
-            fresh0_copy((me + k) % PLANE, 1).wait_send()
-            fresh0_copy((me + k) % PLANE, 0).wait_send()
+    for gives, crossing in ((gives_cross0, 1), (gives_fresh0, 0)):
+        @pl.when(gives)
+        def _():
+            @pl.loop(1, PLANE)
+            def _(k):
+                fresh0_copy((me + k) % PLANE, crossing).wait_send()
 
     @pl.when(relays_fresh0)
     def _():
         fresh0_z.wait_send()
 
-    meta_copy.wait_send()
+    for copy in meta_copies:
+        copy.wait_send()
     zrow_copy.wait_send()
 
-    @pl.loop(0, 8)
-    def _(i):
+    for i in range(6, 8):
         z_copy(i).wait_send()
 
     for group in range(4):
         sum_copy(group).wait_send()
     for sweep, (x_ref, k_ref) in enumerate(((x0, k0), (x1, k1))):
-        for copy in halo_copies(sweep, x_ref, k_ref):
-            copy.wait_send()
+        wait_halo_sent(sweep, x_ref, k_ref)
 
     @pl.loop(0, FRAMES)
     def _(frame):
-        back_copy(frame).wait_send()
+        wait_bytes(ys.at[slot(frame)], s_back.at[frame])
+
+    @pl.when(q % 4 == 0)
+    def _():
+        for i in range(RELAYED):
+            onward_copy(i).wait_send()
 
 
 def local(state, fresh, frame_level, request, q_table, k_table, step_size, reference_kv):
-    meta = jnp.concatenate(
-        [
-            jnp.broadcast_to(frame_level[:, :, None], (2, FRAMES, 128)),
-            jnp.broadcast_to(request[:, :, None], (2, 8, 128)),
-        ],
-        axis=1,
-    )
-    step_tab = jnp.pad(step_size, (0, 128 - step_size.shape[0]))[None, :]
     block = FRAMES * FT
     dma = pltpu.SemaphoreType.DMA
     vmem = pl.BlockSpec(memory_space=pltpu.VMEM)
     return pl.pallas_call(
         kernel,
         out_shape=jax.ShapeDtypeStruct(state.shape, state.dtype),
-        in_specs=[vmem] * 7,
+        in_specs=[pl.BlockSpec(memory_space=pltpu.HBM)] * 8,
         out_specs=vmem,
         scratch_shapes=[
             pltpu.VMEM((HALF, HD), BF16),
@@ -593,8 +699,14 @@
             pltpu.VMEM((4, 8, 128), F32),
             pltpu.VMEM((4, 8, 128), F32),
             pltpu.VMEM((4, PLANE, 8, 128), F32),
-            pltpu.VMEM((24, 128), jnp.int32),
+            pltpu.VMEM(frame_level.shape, jnp.int32),
+            pltpu.VMEM(frame_level.shape, jnp.int32),
+            pltpu.VMEM(request.shape, jnp.int32),
+            pltpu.VMEM(request.shape, jnp.int32),
             pltpu.VMEM((2, 128, WIDTH), F32),
+            pltpu.VMEM((1, step_size.shape[0]), F32),
+            pltpu.VMEM(reference_kv.shape, BF16),
+            pltpu.VMEM((128, 128), F32),
             pltpu.VMEM((2, FRAMES, WIDTH), F32),
             pltpu.VMEM((2, FRAMES, WIDTH), F32),
             pltpu.VMEM((2, FRAMES, WIDTH), F32),
@@ -602,14 +714,15 @@
             pltpu.VMEM((2, FT, WIDTH), BF16),
             dma((PLANE,)), dma((PLANE,)), dma((PLANE,)), dma((PLANE,)), dma((PLANE,)), dma((PLANE,)),
             dma((8,)), dma((8,)), dma, dma,
-            dma((2, 4)), dma((2, 4)), dma, dma, dma((4,)), dma((4,)), dma((4, PLANE)), dma((4, PLANE)),
+            dma((2, 4)), dma((2, 4)), dma((2,)), dma((2,)), dma((4,)), dma((4,)), dma((4, PLANE)), dma((4, PLANE)),
             dma((FRAMES,)), dma((2, 8)), dma((2, PLANE)), dma((2, PLANE)),
             dma((PLANE,)), dma((2,)), dma((PLANE,)), dma((2,)), dma, dma,
+            dma((7,)), pltpu.VMEM((RELAYED * FT, WIDTH), BF16), dma((RELAYED,)), dma((RELAYED,)),
         ],
         compiler_params=pltpu.CompilerParams(
-            collective_id=0, has_side_effects=True, vmem_limit_bytes=48 << 20
+            collective_id=0, has_side_effects=True, vmem_limit_bytes=60 << 20
         ),
-    )(state, fresh[0], meta, q_table, k_table, step_tab, reference_kv)
+    )(state, fresh[0], frame_level, request, q_table, k_table, step_size[None, :], reference_kv)
 
 
 def solution(mesh):

time: 208 us -> 168 us (0.81)
  the two profiles are of different devices: /device:TPU:132 before, /device:TPU:236 now
where the time goes in v2:
time: 168 us
  Pallas kernels  164 us (98%)
  local copies, waits for them, and re-layouts  3.59 us (2%)
    pallas_call x1, Pallas kernels, local(): pl.pallas_call(kernel, out_shape=jax.ShapeDtypeStruct(state.shape, state....  164 us
    unnamed x4, local copies, waits for them, and re-layouts  3.59 us

profile of v2, /device:TPU:236, one launch (start us, length us, event | category | flops | bytes accessed | tf_op | source)
XLA Modules:
  0.0 167.5 jit_solution(15491029012451191410)
XLA Ops:
  0.0 0.0 copy-start
  0.0 0.7 copy-done
  0.7 0.6 copy.9.request
  1.3 163.9 %shard_map.82 = bf16[128,4096]{1,0:T(8,128)(2,1)} custom-call(bf16[128,4096]{1,0:T(8,128)(2,1)} %state.1, bf16[128,4096]{1,0:T(8,128)(2,1)} %bitcast.2, s32[2,16]{1,0:T(2,128)} %frame_level.1, s32[2,1]{1,0:T(2,128)} %copy.9.request, f32[48,128]{1,0:T(8,128)} %q_tab.1, f32[48,128]{1,0:T(8,128)} %k_tab.1, f32[1,48]{1,0:T(1,128)} %bitcast.3, ...), custom_call_target="tpu_custom_call" | custom-call | tf_op jit(solution)/shard_map/pallas_call | solution.py:678
  165.2 2.3 %copy.11 = bf16[128,4096]{1,0:T(8,128)(2,1)} copy(bf16[128,4096]{1,0:T(8,128)(2,1)} %shard_map.82) | data formatting | bytes 2097152
Async XLA Ops:
  0.0 0.7 copy-start

commit v3 on v2

--- a/solution.py
+++ b/solution.py
@@ -569,21 +569,20 @@
     prepare_pair(6)
     first_pairs(5, 1)
     start_sums(2)
-    wait_halo(1, x1, k1)
-    second_pairs(0, 1)
     arrive(7)
     prepare_pair(7)
     first_pairs(6, 2)
     start_sums(3)
+    spread_sums(2)
+    spread_sums(3)
+    wait_halo(1, x1, k1)
+    second_pairs(0, 1)
     prepare_group(1)
-    second_pairs(1, 1)
-    spread_sums(2)
+    second_pairs(1, 2)
     relay_back(0)
-    second_pairs(2, 1)
-    spread_sums(3)
-    relay_back(1)
     prepare_group(2)
     second_pairs(3, 2)
+    relay_back(1)
     relay_back(2)
     prepare_group(3)
     second_pairs(5, 3)

time: 168 us -> 160 us (0.952)
  the two profiles are of different devices: /device:TPU:236 before, /device:TPU:196 now
where the time goes in v3:
time: 160 us
  Pallas kernels  156 us (98%)
  local copies, waits for them, and re-layouts  3.59 us (2%)
    pallas_call x1, Pallas kernels, local(): pl.pallas_call(kernel, out_shape=jax.ShapeDtypeStruct(state.shape, state....  156 us
    unnamed x4, local copies, waits for them, and re-layouts  3.59 us

profile of v3, /device:TPU:196, one launch (start us, length us, event | category | flops | bytes accessed | tf_op | source)
XLA Modules:
  0.0 159.9 jit_solution(12766926780254276116)
XLA Ops:
  0.0 0.0 copy-start
  0.0 0.7 copy-done
  0.7 0.6 copy.9.request
  1.3 156.3 %shard_map.82 = bf16[128,4096]{1,0:T(8,128)(2,1)} custom-call(bf16[128,4096]{1,0:T(8,128)(2,1)} %state.1, bf16[128,4096]{1,0:T(8,128)(2,1)} %bitcast.2, s32[2,16]{1,0:T(2,128)} %frame_level.1, s32[2,1]{1,0:T(2,128)} %copy.9.request, f32[48,128]{1,0:T(8,128)} %q_tab.1, f32[48,128]{1,0:T(8,128)} %k_tab.1, f32[1,48]{1,0:T(1,128)} %bitcast.3, ...), custom_call_target="tpu_custom_call" | custom-call | tf_op jit(solution)/shard_map/pallas_call | solution.py:677
  157.6 2.3 %copy.11 = bf16[128,4096]{1,0:T(8,128)(2,1)} copy(bf16[128,4096]{1,0:T(8,128)(2,1)} %shard_map.82) | data formatting | bytes 2097152
Async XLA Ops:
  0.0 0.7 copy-start
